TPU v7x, 32 devices: a whole 2x2x4 slice. The times are simulated.
32 devices in a mesh: section: 8 (over y, x, core), expert: 4 (over z).
Axes of the slice: x: 2, y: 2, z: 4, core: 2. Of those that a mesh axis runs over, the one named last changes fastest.
Arguments:
- tokens: bfloat16 [8, 512, 7168], P('section', 'expert'), may hold values from -6 to 6
- cotangent: bfloat16 [8, 512, 7168], P('section', 'expert'), may hold values from -6 to 6
- expert_ids: int32 [8, 512, 8], P('section', 'expert'), may hold values from 0 to 31, as said below
- slot_index: int32 [8, 512, 8], P('section', 'expert'), may hold values from 0 to 31, as said below
- gate_scale: float32 [8, 512, 8], P('section', 'expert'), may hold values from 0.2 to 1.2
- gate_weight: bfloat16 [8, 7168, 2048], P('section', None, 'expert'), may hold values from -0.0625 to 0.0625
- up_weight: bfloat16 [8, 7168, 2048], P('section', None, 'expert'), may hold values from -0.0625 to 0.0625
- down_weight: bfloat16 [8, 2048, 7168], P('section', 'expert'), may hold values from -0.125 to 0.125
Outputs:
- next_input: bfloat16 [8, 512, 7168], P('section', 'expert')
- prior_grad: bfloat16 [8, 512, 7168], P('section', 'expert')
Inputs may be any that keep to these rules, and one draw needn't show every extreme that they name: `expert_ids`: each token names 8 different experts; among the 128 tokens of one device every expert is named exactly 32 times. `slot_index`: among the routes of one device's tokens to one expert, the slots are 0 to 31, each once.
All inputs are finite; a program needn't handle non-finite values.
Results may differ from a plain program's by a relative error of at most 0.011.
Values may be sent and summed in bfloat16 or wider, within the bound.
A program may use at most 128 MiB of HBM per device.

v0:
```python
import jax
import jax.numpy as jnp
from jax import lax
from jax.sharding import PartitionSpec as P

CAP = 32


def from_behind(x, axis, by):
    length = lax.axis_size(axis)
    pairs = [(i, i + by) for i in range(length) if 0 <= i + by < length]
    return lax.ppermute(x, axis, pairs)


def silu_parts(gate):
    sig = jax.nn.sigmoid(gate)
    return (gate * sig, sig * (1.0 + gate * (1.0 - sig)))


def body(
    tokens, cotangent, expert_ids, slot_index, gate_scale, gate_weight, up_weight, down_weight
):
    section = lax.axis_index("section")
    local = tokens[0]
    grad_out = cotangent[0]
    named = expert_ids[0]
    gate_mat = gate_weight[0]
    up_mat = up_weight[0]
    down_mat = down_weight[0]
    width_local = gate_mat.shape[1]
    hit = named == section
    chosen = jnp.any(hit, axis=1)
    slot = jnp.sum(jnp.where(hit, slot_index[0], 0), axis=1)
    weight = jnp.sum(jnp.where(hit, gate_scale[0], jnp.float32(0.0)), axis=1)
    places = jnp.arange(CAP, dtype=jnp.int32)
    table = ((places[:, None] == slot[None, :]) & chosen[None, :]).astype(jnp.bfloat16)
    sent = jnp.dot(table, local, preferred_element_type=jnp.float32).astype(jnp.bfloat16)
    carried = (weight[:, None] * grad_out.astype(jnp.float32)).astype(jnp.bfloat16)
    back = jnp.dot(table, carried, preferred_element_type=jnp.float32).astype(jnp.bfloat16)
    piece = lax.all_gather(sent, "expert", axis=0, tiled=True)
    gate_up = jnp.concatenate(
        [
            jnp.dot(piece, gate_mat, preferred_element_type=jnp.float32),
            jnp.dot(piece, up_mat, preferred_element_type=jnp.float32),
        ],
        axis=1,
    )
    gate = gate_up[:, :width_local]
    up = gate_up[:, width_local:]
    act, slope = silu_parts(gate)
    hidden = (act * up).astype(jnp.bfloat16)
    combined = lax.psum_scatter(
        jnp.dot(hidden, down_mat, preferred_element_type=jnp.float32).astype(jnp.bfloat16),
        "expert",
        scatter_dimension=0,
        tiled=True,
    ).astype(jnp.float32)
    grad_hidden = jnp.dot(
        lax.all_gather(back, "expert", axis=0, tiled=True),
        down_mat.T,
        preferred_element_type=jnp.float32,
    )
    grad_up = (grad_hidden * act).astype(jnp.bfloat16)
    grad_gate = (grad_hidden * up * slope).astype(jnp.bfloat16)
    behind = jnp.dot(grad_gate, gate_mat.T, preferred_element_type=jnp.float32)
    inward = lax.psum_scatter(
        (behind + jnp.dot(grad_up, up_mat.T, preferred_element_type=jnp.float32)).astype(
            jnp.bfloat16
        ),
        "expert",
        scatter_dimension=0,
        tiled=True,
    ).astype(jnp.float32)
    output = local.astype(jnp.float32) + weight[:, None] * jnp.take(combined, slot, axis=0)
    grad_in = grad_out.astype(jnp.float32) + jnp.where(
        chosen[:, None], jnp.take(inward, slot, axis=0), jnp.float32(0.0)
    )
    next_input = from_behind(output.astype(jnp.bfloat16)[None], "section", 1)
    prior_grad = from_behind(grad_in.astype(jnp.bfloat16)[None], "section", -1)
    return (next_input, prior_grad)


def solution(mesh):
    in_specs = (
        P("section", "expert", None),
        P("section", "expert", None),
        P("section", "expert", None),
        P("section", "expert", None),
        P("section", "expert", None),
        P("section", None, "expert"),
        P("section", None, "expert"),
        P("section", "expert", None),
    )
    out_specs = (P("section", "expert", None), P("section", "expert", None))
    return jax.shard_map(body, mesh=mesh, in_specs=in_specs, out_specs=out_specs, check_vma=False)
```

profile of v0, /device:TPU:1, one launch (start us, length us, event | category | flops | bytes accessed | tf_op | source)
XLA Modules:
  0.0 238.7 jit_solution(635253242369340927)
XLA Ops:
  7.2 0.0 all-gather.3.cloned.1.call-start
  7.2 0.7 select_reduce_fusion.1
  7.9 0.7 select_reduce_fusion
  8.7 2.6 %convolution_convert_fusion.2 = bf16[32,7168]{1,0:T(8,128)(2,1)} fusion(bf16[1,128,7168]{2,1,0:T(8,128)(2,1)} %param.10, s32[128]{0:T(128)S(1)} %select_reduce_fusion, pred[128]{0:T(512)(128)(4,1)S(1)} %reduce_or.9), kind=kOutput, calls=%fused_computation.6 | convolution fusion | flops 58957824 | bytes 2294400 | tf_op jit(solution)/shard_map/dot_general | solution.py:37
  11.3 0.0 all-gather.3.cloned.1.call-update
  11.3 0.0 all-gather.5.cloned.1.call-start
  11.4 2.8 %convolution_convert_fusion.1 = bf16[32,7168]{1,0:T(8,128)(2,1)} fusion(bf16[1,128,7168]{2,1,0:T(8,128)(2,1)} %param.11, f32[128]{0:T(128)S(1)} %get-tuple-element.3, s32[128]{0:T(128)S(1)} %select_reduce_fusion, pred[128]{0:T(512)(128)(4,1)S(1)} %reduce_or.9), kind=kOutput, calls=%fused_computation.5 | convolution fusion | flops 61710336 | bytes 2294912 | tf_op jit(solution)/shard_map/dot_general | solution.py:39
  14.1 0.0 all-gather.5.cloned.1.call-update
  14.2 0.0 reduce-scatter.3.cloned.1.call-start
  14.2 40.7 %all-gather.3.cloned.1.call-done = bf16[128,7168]{1,0:T(8,128)(2,1)} async-done(((bf16[32,7168]{1,0:T(8,128)(2,1)}), bf16[128,7168]{1,0:T(8,128)(2,1)}) %all-gather.3.cloned.1.call-update) | async-done | bytes 1835024 | tf_op jit(solution)/shard_map/all_gather | solution.py:40
  55.0 0.0 copy-start
  55.0 0.0 slice-start.2
  55.0 4.9 %fusion.9 = f32[128,512]{1,0:T(8,128)S(1)} fusion(bf16[128,7168]{1,0:T(8,128)(2,1)} %all-gather.3.cloned.1.call-done, bf16[1,7168,512]{2,1,0:T(8,128)(2,1)} %param.15), kind=kOutput, calls=%fused_computation.15 | convolution fusion | flops 939524096 | bytes 9437184 | tf_op jit(solution)/shard_map/dot_general | solution.py:43
  59.9 0.0 copy-done
  59.9 0.0 slice-start.3
  59.9 4.5 %fusion.5 = f32[128,512]{1,0:T(8,128)S(1)} fusion(bf16[128,7168]{1,0:T(8,128)(2,1)S(1)} %copy-done, bf16[1,7168,512]{2,1,0:T(8,128)(2,1)} %param.16), kind=kOutput, calls=%fused_computation.11 | convolution fusion | flops 939524096 | bytes 9437184 | tf_op jit(solution)/shard_map/dot_general | solution.py:44
  64.4 0.0 slice-done.2
  64.4 0.0 slice-done.3
  64.4 2.4 %convolution_convert_fusion = bf16[128,7168]{1,0:T(8,128)(2,1)} fusion(bf16[1,512,7168]{2,1,0:T(8,128)(2,1)S(1)} %bitcast.36, f32[128,512]{1,0:T(8,128)S(1)} %fusion.5, f32[128,512]{1,0:T(8,128)S(1)} %fusion.9), kind=kOutput, calls=%fused_computation.4 | convolution fusion | flops 940834816 | bytes 9699328 | tf_op jit(solution)/shard_map/dot_general | solution.py:53
  66.8 0.0 reduce-scatter.3.cloned.1.call-update
  66.9 0.2 reduce-scatter.5.cloned.1.call-start
  67.1 29.7 %all-gather.5.cloned.1.call-done = bf16[128,7168]{1,0:T(8,128)(2,1)} async-done(((bf16[32,7168]{1,0:T(8,128)(2,1)}), bf16[128,7168]{1,0:T(8,128)(2,1)}) %all-gather.5.cloned.1.call-update) | async-done | bytes 1835024 | tf_op jit(solution)/shard_map/all_gather | solution.py:59
  96.8 0.0 slice-start
  96.8 6.4 %fusion.1 = f32[128,512]{1,0:T(8,128)S(1)} fusion(bf16[128,7168]{1,0:T(8,128)(2,1)} %all-gather.5.cloned.1.call-done, bf16[1,512,7168]{2,1,0:T(8,128)(2,1)} %param.17), kind=kOutput, calls=%fused_computation.7 | convolution fusion | flops 939524096 | bytes 9437184 | tf_op jit(solution)/shard_map/dot_general | solution.py:58
  103.2 0.0 slice-start.1
  103.2 6.1 %fusion.7 = f32[128,7168]{1,0:T(8,128)S(1)} fusion(bf16[1,7168,512]{2,1,0:T(8,128)(2,1)} %param.15, f32[128,512]{1,0:T(8,128)S(1)} %fusion.9, f32[128,512]{1,0:T(8,128)S(1)} %fusion.1, f32[128,512]{1,0:T(8,128)S(1)} %fusion.5), kind=kOutput, calls=%fused_computation.13 | convolution fusion | flops 940179456 | bytes 11796480 | tf_op jit(solution)/shard_map/dot_general | solution.py:65
  109.3 0.0 slice-done
  109.3 0.0 slice-done.1
  109.3 3.7 %fusion = bf16[128,7168]{1,0:T(8,128)(2,1)} fusion(f32[128,7168]{1,0:T(8,128)S(1)} %fusion.7, bf16[1,7168,512]{2,1,0:T(8,128)(2,1)S(1)} %bitcast.34, f32[128,512]{1,0:T(8,128)S(1)} %fusion.1, f32[128,512]{1,0:T(8,128)S(1)} %fusion.9), kind=kOutput, calls=%fused_computation.3 | convolution fusion | flops 941752320 | bytes 13369344 | tf_op jit(solution)/shard_map/dot_general | solution.py:67
  113.0 0.0 reduce-scatter.5.cloned.1.call-update
  113.1 24.8 %reduce-scatter.3.cloned.1.call-done = bf16[32,7168]{1,0:T(8,128)(2,1)} async-done(((bf16[128,7168]{1,0:T(8,128)(2,1)}), bf16[32,7168]{1,0:T(8,128)(2,1)}) %reduce-scatter.3.cloned.1.call-update) | async-done | bytes 458768 | tf_op jit(solution)/shard_map/reduce_scatter | solution.py:52
  137.9 1.1 convert_element_type.51
  138.9 3.4 %gather_fusion = f32[128,7168]{1,0:T(8,128)} fusion(f32[32,7168]{1,0:T(8,128)S(1)} %convert_element_type.51, s32[1024]{0:T(1024)S(1)} %pad_clamp_fusion), kind=kCustom, calls=%fused_computation.clone | custom fusion | bytes 7340544 | tf_op jit(solution)/shard_map/jit(_take)/gather | solution.py:74
  142.4 36.8 %reduce-scatter.5.cloned.1.call-done = bf16[32,7168]{1,0:T(8,128)(2,1)} async-done(((bf16[128,7168]{1,0:T(8,128)(2,1)}), bf16[32,7168]{1,0:T(8,128)(2,1)}) %reduce-scatter.5.cloned.1.call-update) | async-done | bytes 458768 | tf_op jit(solution)/shard_map/reduce_scatter | solution.py:66
  179.2 1.1 convert_element_type.60
  180.3 0.0 copy-start.1
  180.3 3.5 %gather_fusion.1 = f32[128,7168]{1,0:T(8,128)} fusion(f32[32,7168]{1,0:T(8,128)S(1)} %convert_element_type.60, s32[1024]{0:T(1024)S(1)} %pad_clamp_fusion), kind=kCustom, calls=%fused_computation.1.clone | custom fusion | bytes 7340544 | tf_op jit(solution)/shard_map/jit(_take)/gather | solution.py:76
  183.7 0.0 copy-done.1
  183.7 5.2 %fusion.16 = (bf16[1,128,7168]{2,1,0:T(8,128)(2,1)S(1)}, bf16[1,128,7168]{2,1,0:T(8,128)(2,1)S(1)}) fusion(f32[128,7168]{1,0:T(8,128)} %gather_fusion.1, bf16[1,128,7168]{2,1,0:T(8,128)(2,1)} %param.11, pred[128]{0:T(512)(128)(4,1)S(1)} %compare_and_fusion, pred[128]{0:T(512)(128)(4,1)S(1)} %reduce_or.9, f32[128,7168]{1,0:T(8,128)} %gather_fusion, ...), kind=kLoop, calls=%fused_computation.26 | loop fusion | flops 9175040 | bytes 14680832 | tf_op jit(solution)/shard_map/broadcast_in_dim | solution.py:79
  189.0 2.7 %collective-permute-start.1 = (bf16[1,128,7168]{2,1,0:T(8,128)(2,1)S(1)}, bf16[1,128,7168]{2,1,0:T(8,128)(2,1)S(1)}, u32[]{:S(2)}, u32[]{:S(2)}) collective-permute-start(bf16[1,128,7168]{2,1,0:T(8,128)(2,1)S(1)} %get-tuple-element.5), channel_id=1, source_target_pairs={{4,0},{8,4},{12,8},{16,12},{20,16},{24,20},{28,24},{5,1},{9,5},{13... | collective-permute-start | bytes 5505032 | tf_op jit(solution)/shard_map/ppermute | solution.py:12
  191.7 3.0 %collective-permute-start = (bf16[1,128,7168]{2,1,0:T(8,128)(2,1)S(1)}, bf16[1,128,7168]{2,1,0:T(8,128)(2,1)S(1)}, u32[]{:S(2)}, u32[]{:S(2)}) collective-permute-start(bf16[1,128,7168]{2,1,0:T(8,128)(2,1)S(1)} %get-tuple-element.6), channel_id=1, source_target_pairs={{0,4},{4,8},{8,12},{12,16},{16,20},{20,24},{24,28},{1,5},{5,9},{9,... | collective-permute-start | bytes 5505032 | tf_op jit(solution)/shard_map/ppermute | solution.py:12
  194.7 35.0 %collective-permute-done.1 = bf16[1,128,7168]{2,1,0:T(8,128)(2,1)S(1)} collective-permute-done((bf16[1,128,7168]{2,1,0:T(8,128)(2,1)S(1)}, bf16[1,128,7168]{2,1,0:T(8,128)(2,1)S(1)}, u32[]{:S(2)}, u32[]{:S(2)}) %collective-permute-start.1) | collective-permute-done | bytes 1835040 | tf_op jit(solution)/shard_map/ppermute | solution.py:12
  229.7 0.0 collective-permute-done
  229.7 1.2 copy.12
  230.9 1.2 copy.13
  (6 shorter events, 0.0 us)
Async XLA Ops:
  7.2 47.8 %all-gather.3.cloned.1.call-start = ((), (), s32[]{:S(2)}) async-start(), calls=%async_computation.2 | async-start | bytes 2293760 | tf_op jit(solution)/shard_map/all_gather | solution.py:40
  11.3 85.5 %all-gather.5.cloned.1.call-start = ((), (), s32[]{:S(2)}) async-start(), calls=%async_computation.4 | async-start | bytes 2293760 | tf_op jit(solution)/shard_map/all_gather | solution.py:59
  14.2 123.7 %reduce-scatter.3.cloned.1.call-start = ((), (), s32[]{:S(2)}) async-start(), calls=%async_computation.3 | async-start | bytes 2293760 | tf_op jit(solution)/shard_map/reduce_scatter | solution.py:52
  55.0 4.9 %copy-start = (bf16[128,7168]{1,0:T(8,128)(2,1)S(1)}, bf16[128,7168]{1,0:T(8,128)(2,1)}, u32[]{:S(2)}) copy-start(bf16[128,7168]{1,0:T(8,128)(2,1)} %all-gather.3.cloned.1.call-done) | copy-start | bytes 5505028
  55.0 9.4 %slice-start.2 = ((s8[7340032]{0:T(1024)(128)(4,1)}), s8[4194304]{0:T(1024)(128)(4,1)S(1)}, s32[]{:S(2)}) async-start(s8[7340032]{0:T(1024)(128)(4,1)} %bitcast.35), calls=%async_computation.8 | async-start | bytes 8388608
  59.9 4.5 %slice-start.3 = ((s8[7340032]{0:T(1024)(128)(4,1)}), s8[3145728]{0:T(1024)(128)(4,1)S(1)}, s32[]{:S(2)}) async-start(s8[7340032]{0:T(1024)(128)(4,1)} %bitcast.35), calls=%async_computation.9 | async-start | bytes 6291456
  66.9 112.3 %reduce-scatter.5.cloned.1.call-start = ((), (), s32[]{:S(2)}) async-start(), calls=%async_computation.5 | async-start | bytes 2293760 | tf_op jit(solution)/shard_map/reduce_scatter | solution.py:66
  96.8 12.5 %slice-start = ((s8[7340032]{0:T(1024)(128)(4,1)}), s8[4194304]{0:T(1024)(128)(4,1)S(1)}, s32[]{:S(2)}) async-start(s8[7340032]{0:T(1024)(128)(4,1)} %bitcast.33), calls=%async_computation.6 | async-start | bytes 8388608
  103.2 6.1 %slice-start.1 = ((s8[7340032]{0:T(1024)(128)(4,1)}), s8[3145728]{0:T(1024)(128)(4,1)S(1)}, s32[]{:S(2)}) async-start(s8[7340032]{0:T(1024)(128)(4,1)} %bitcast.33), calls=%async_computation.7 | async-start | bytes 6291456
  180.3 3.5 %copy-start.1 = (bf16[1,128,7168]{2,1,0:T(8,128)(2,1)S(1)}, bf16[1,128,7168]{2,1,0:T(8,128)(2,1)}, u32[]{:S(2)}) copy-start(bf16[1,128,7168]{2,1,0:T(8,128)(2,1)} %param.10) | copy-start | bytes 5505028
  189.0 40.7 %collective-permute-start.1 = (bf16[1,128,7168]{2,1,0:T(8,128)(2,1)S(1)}, bf16[1,128,7168]{2,1,0:T(8,128)(2,1)S(1)}, u32[]{:S(2)}, u32[]{:S(2)}) collective-permute-start(bf16[1,128,7168]{2,1,0:T(8,128)(2,1)S(1)} %get-tuple-element.5), channel_id=1, source_target_pairs={{4,0},{8,4},{12,8},{16,12},{20,16},{24,20},{28,24},{5,1},{9,5},{13... | collective-permute-start | bytes 5505032 | tf_op jit(solution)/shard_map/ppermute | solution.py:12
  191.7 38.0 %collective-permute-start = (bf16[1,128,7168]{2,1,0:T(8,128)(2,1)S(1)}, bf16[1,128,7168]{2,1,0:T(8,128)(2,1)S(1)}, u32[]{:S(2)}, u32[]{:S(2)}) collective-permute-start(bf16[1,128,7168]{2,1,0:T(8,128)(2,1)S(1)} %get-tuple-element.6), channel_id=1, source_target_pairs={{0,4},{4,8},{8,12},{12,16},{16,20},{20,24},{24,28},{1,5},{5,9},{9,... | collective-permute-start | bytes 5505032 | tf_op jit(solution)/shard_map/ppermute | solution.py:12
Sparse Core Ops, SparseCore 0:
  11.4 43.4 all-gather.2
  56.5 40.2 all-gather.4
  99.7 38.1 reduce-scatter.2
  140.6 38.5 reduce-scatter.4
where the time goes:
time: 242 us; the launch traced here: 239 us
  waiting for transfers between devices  167 us (69%)
  matrix products  33.4 us (14%)
  between operations  13.9 us (6%)
  local copies, waits for them, and re-layouts  9.41 us (4%)
  other arithmetic  8.83 us (4%)
  starting transfers between devices  6.06 us (3%)
    all_gather x1, waiting for transfers between devices, body(): piece = lax.all_gather(sent, 'expert', axis=0, tiled=True)  40.7 us
    reduce_scatter x1, waiting for transfers between devices, body(): lax.psum_scatter((behind + jnp.dot(grad_up, up_mat.T, preferred_element_t...  36.8 us
    ppermute x2, waiting for transfers between devices, from_behind(): return lax.ppermute(x, axis, pairs)  35 us
    all_gather x1, waiting for transfers between devices, body(): lax.all_gather(back, 'expert', axis=0, tiled=True)  29.7 us
    reduce_scatter x1, waiting for transfers between devices, body(): lax.psum_scatter(jnp.dot(hidden, down_mat, preferred_element_type=jnp.flo...  24.8 us
    dot_general x1, matrix products, body(): jnp.dot(lax.all_gather(back, 'expert', axis=0, tiled=True), down_mat.T, p...  6.36 us
    dot_general x1, matrix products, body(): behind = jnp.dot(grad_gate, gate_mat.T, preferred_element_type=jnp.float32)  6.07 us
    ppermute x2, starting transfers between devices, from_behind(): return lax.ppermute(x, axis, pairs)  5.72 us
  transfers between devices with their start and end apart: 6, of which 5 were waited for; matrix products, arithmetic and copies ran while one was open for 15% of the time, Pallas kernels for 0%

commit v1 on v0

v1 whole, which is shorter than its diff:
```python
import functools

import jax
import jax.numpy as jnp
from jax import lax
from jax.experimental import pallas as pl
from jax.experimental.pallas import tpu as pltpu
from jax.sharding import PartitionSpec as P

CAP = 32
CH = 1024
PIECES = 2
MESH = pl.DeviceIdType.MESH
NT = (((1,), (1,)), ((), ()))
TN = (((0,), (0,)), ((), ()))


def kernel(
    n,
    n_sec,
    ids_ref,
    slots_ref,
    scale_ref,
    tok_hbm,
    cot_hbm,
    gw_hbm,
    uw_hbm,
    dw_hbm,
    next_hbm,
    prior_hbm,
    tok,
    cot,
    gw,
    uw,
    dw,
    gs,
    gb,
    rs_in,
    fin,
    shift,
    route,
    route_in,
    gate,
    up,
    hid,
    load_sem,
    ag_send,
    ag_recv,
    rs_send,
    rs_recv,
    fin_send,
    fin_recv,
    shift_send,
    shift_recv,
    route_send,
    route_recv,
    out_sem,
):
    f32, bf16 = jnp.float32, jnp.bfloat16
    sec = lax.axis_index("section")
    me = lax.axis_index("expert")
    d = tok.shape[1]
    nc = d // CH
    pw = d // PIECES
    has_right, has_left = me < n - 1, me > 0
    has_next, has_prev = sec < n_sec - 1, sec > 0
    right = (sec, jnp.minimum(me + 1, n - 1))
    left = (sec, jnp.maximum(me - 1, 0))
    after = (jnp.minimum(sec + 1, n_sec - 1), me)
    before = (jnp.maximum(sec - 1, 0), me)
    neighbours = ((has_right, right), (has_left, left), (has_next, after), (has_prev, before))
    bufs = (gs, gb)

    loads = [
        pltpu.make_async_copy(src, dst, load_sem.at[k])
        for k, (src, dst) in enumerate(
            ((tok_hbm, tok), (cot_hbm, cot), (gw_hbm, gw), (uw_hbm, uw), (dw_hbm, dw))
        )
    ]
    for load in loads:
        load.start()

    barrier = pltpu.get_barrier_semaphore()
    for exists, where in neighbours:

        @pl.when(exists)
        def _():
            pl.semaphore_signal(barrier, inc=1, device_id=where, device_id_type=MESH)

    def col(c):
        return pl.ds(pl.multiple_of(c * CH, CH), CH)

    hit = ids_ref[...] == sec
    slot = jnp.sum(jnp.where(hit, slots_ref[...], 0), axis=1, keepdims=True)
    weight = jnp.sum(jnp.where(hit, scale_ref[...], 0.0), axis=1, keepdims=True)
    chosen = jnp.sum(hit.astype(jnp.int32), axis=1, keepdims=True)
    lane = lax.broadcasted_iota(jnp.int32, (hit.shape[0], 128), 1)
    picks = jnp.where((lane == slot) & (chosen > 0), 1.0, 0.0)
    route[...] = jnp.where(lane < CAP, picks, weight)

    def gather_own(a):
        @pl.loop(0, nc)
        def _(c):
            table = route[:, :CAP].astype(bf16)
            if a == 0:
                rows = tok[:, col(c)]
            else:
                rows = (route[:, CAP : CAP + 1] * cot[:, col(c)].astype(f32)).astype(bf16)
            got = lax.dot_general(table, rows, TN, preferred_element_type=f32)
            bufs[a][me, :, col(c)] = got.astype(bf16)

    def ag_copy(a, j, p, way):
        ref = bufs[a].at[j, :, pl.ds(p * pw, pw)]
        return pltpu.make_async_remote_copy(
            src_ref=ref,
            dst_ref=ref,
            send_sem=ag_send.at[a, way, j, p],
            recv_sem=ag_recv.at[a, j, p],
            device_id=(right, left)[way],
            device_id_type=MESH,
        )

    def ag_step(a, s):
        for way, j, ok in ((0, me - s, me - s >= 0), (1, me + s, me + s < n)):
            for p in range(PIECES):

                @pl.when(ok)
                def _():
                    if s > 0:
                        ag_copy(a, j, p, way).wait_recv()
                    if s < n - 1:

                        @pl.when((has_right, has_left)[way])
                        def _():
                            ag_copy(a, j, p, way).start()

    def ag_sent(a):
        for s in range(n - 1):
            for way, j, ok in ((0, me - s, me - s >= 0), (1, me + s, me + s < n)):

                @pl.when(ok & (has_right, has_left)[way])
                def _():
                    for p in range(PIECES):
                        ag_copy(a, j, p, way).wait_send()

    def rs_copy(a, j, c, way):
        into = j if way == 0 else jnp.where(j == me - 1, n, j)
        return pltpu.make_async_remote_copy(
            src_ref=bufs[a].at[j, :, col(c)],
            dst_ref=rs_in.at[a, into, :, col(c)],
            send_sem=rs_send.at[a, j, c],
            recv_sem=rs_recv.at[a, into, c],
            device_id=(right, left)[way],
            device_id_type=MESH,
        )

    def rs_take(a, j, into, c):
        pltpu.make_async_remote_copy(
            src_ref=bufs[a].at[j, :, col(c)],
            dst_ref=rs_in.at[a, into, :, col(c)],
            send_sem=rs_send.at[a, j, c],
            recv_sem=rs_recv.at[a, into, c],
            device_id=right,
            device_id_type=MESH,
        ).wait_recv()
        total = bufs[a][j, :, col(c)].astype(f32) + rs_in[a, into, :, col(c)].astype(f32)
        bufs[a][j, :, col(c)] = total.astype(bf16)

    def rs_first(a, c):
        for s in range(n - 1):

            @pl.when(me == 0)
            def _():
                rs_copy(a, n - 1 - s, c, 0).start()

            @pl.when(me == n - 1)
            def _():
                rs_copy(a, s, c, 1).start()

    def fin_copy(a, c):
        return pltpu.make_async_remote_copy(
            src_ref=bufs[a].at[me, :, col(c)],
            dst_ref=fin.at[a, :, col(c)],
            send_sem=fin_send.at[a, c],
            recv_sem=fin_recv.at[a, c],
            device_id=(after, before)[a],
            device_id_type=MESH,
        )

    def rs_relay(a, c):
        for s in range(n - 1):
            for way, j, ok in (
                (0, n - 1 - s, (n - 1 - s > me) & has_left),
                (1, s, (s < me) & has_right),
            ):

                @pl.when(ok)
                def _():
                    rs_take(a, j, j, c)
                    rs_copy(a, j, c, way).start()

        @pl.when(has_left)
        def _():
            rs_take(a, me, me, c)

        @pl.when(has_right)
        def _():
            rs_take(a, me, n, c)

        @pl.when((has_next, has_prev)[a])
        def _():
            fin_copy(a, c).start()

    def rs_sent(a, c):
        for j in range(n):
            for way, ok in ((0, j > me), (1, j < me)):

                @pl.when(ok)
                def _():
                    rs_copy(a, j, c, way).wait_send()

        @pl.when((has_next, has_prev)[a])
        def _():
            fin_copy(a, c).wait_send()

    def shift_copy(a):
        return pltpu.make_async_remote_copy(
            src_ref=(tok, cot)[a],
            dst_ref=shift.at[a],
            send_sem=shift_send.at[a],
            recv_sem=shift_recv.at[a],
            device_id=(after, before)[a],
            device_id_type=MESH,
        )

    def route_copy(a):
        return pltpu.make_async_remote_copy(
            src_ref=route,
            dst_ref=route_in.at[a],
            send_sem=route_send.at[a],
            recv_sem=route_recv.at[a],
            device_id=(after, before)[a],
            device_id_type=MESH,
        )

    def out_copy(a, c):
        return pltpu.make_async_copy(
            shift.at[a, :, col(c)], (next_hbm, prior_hbm)[a].at[:, col(c)], out_sem.at[a, c]
        )

    sends_on = (has_next, has_prev)
    takes_from = (has_prev, has_next)

    def finish(a, c):
        @pl.when(takes_from[a])
        def _():
            fin_copy(a, c).wait_recv()
            table = route_in[a, :, :CAP].astype(bf16)
            rows = jnp.dot(table, fin[a, :, col(c)], preferred_element_type=f32)
            if a == 0:
                rows = route_in[a, :, CAP : CAP + 1] * rows
            shift[a, :, col(c)] = (shift[a, :, col(c)].astype(f32) + rows).astype(bf16)

        @pl.when(jnp.logical_not(takes_from[a]))
        def _():
            shift[a, :, col(c)] = jnp.zeros((shift.shape[1], CH), bf16)

        out_copy(a, c).start()

    loads[0].wait()
    gather_own(0)
    peers = sum(exists.astype(jnp.int32) for exists, _w in neighbours)
    pl.semaphore_wait(barrier, peers)

    ag_step(0, 0)
    loads[1].wait()
    gather_own(1)
    for a in range(2):

        @pl.when(sends_on[a])
        def _():
            route_copy(a).start()
            shift_copy(a).start()

    for s in range(n):
        if s > 0:
            ag_step(0, s)
        for p in range(PIECES):

            @pl.when((me == s) & has_right)
            def _():
                ag_copy(1, me, p, 0).start()

            @pl.when((me == n - 1 - s) & has_left)
            def _():
                ag_copy(1, me, p, 1).start()

    loads[2].wait()
    loads[3].wait()
    m = n * CAP
    gate[...] = jnp.zeros_like(gate)
    up[...] = jnp.zeros_like(up)

    @pl.loop(0, nc)
    def _(c):
        rows = gs[:, :, col(c)].reshape(m, CH)
        gate[...] += jnp.dot(rows, gw[col(c), :], preferred_element_type=f32)
        up[...] += jnp.dot(rows, uw[col(c), :], preferred_element_type=f32)

    g = gate[...]
    hid[0] = (g * jax.nn.sigmoid(g) * up[...]).astype(bf16)
    loads[4].wait()
    ag_sent(0)

    @pl.loop(0, nc)
    def _(c):
        part = jnp.dot(hid[0], dw[:, col(c)], preferred_element_type=f32)
        gs[:, :, col(c)] = part.astype(bf16).reshape(n, CAP, CH)
        rs_first(0, c)

    for s in range(1, n):
        ag_step(1, s)

    def grad_hidden(c, total):
        rows = gb[:, :, col(c)].reshape(m, CH)
        return total + lax.dot_general(rows, dw[:, col(c)], NT, preferred_element_type=f32)

    gh = lax.fori_loop(0, nc, grad_hidden, jnp.zeros(gate.shape, f32))
    g = gate[...]
    sig = jax.nn.sigmoid(g)
    hid[0] = (gh * (g * sig)).astype(bf16)
    hid[1] = (gh * up[...] * (sig * (1.0 + g * (1.0 - sig)))).astype(bf16)
    ag_sent(1)

    @pl.loop(0, nc)
    def _(c):
        rs_relay(0, c)

    @pl.loop(0, nc)
    def _(c):
        part = lax.dot_general(hid[1], gw[col(c), :], NT, preferred_element_type=f32)
        part += lax.dot_general(hid[0], uw[col(c), :], NT, preferred_element_type=f32)
        gb[:, :, col(c)] = part.astype(bf16).reshape(n, CAP, CH)
        rs_first(1, c)

    for a in range(2):

        @pl.when(takes_from[a])
        def _():
            route_copy(a).wait_recv()
            shift_copy(a).wait_recv()

    @pl.loop(0, nc)
    def _(c):
        rs_relay(1, c)
        finish(0, c)

    @pl.loop(0, nc)
    def _(c):
        finish(1, c)

    for a in range(2):

        @pl.when(sends_on[a])
        def _():
            route_copy(a).wait_send()
            shift_copy(a).wait_send()

    @pl.loop(0, nc)
    def _(c):
        for a in range(2):
            rs_sent(a, c)
            out_copy(a, c).wait()


def body(
    n, n_sec, tokens, cotangent, expert_ids, slot_index, gate_scale, gate_weight, up_weight, down_weight
):
    t, d = tokens.shape[1:]
    h = gate_weight.shape[2]
    nc = d // CH
    m = n * CAP
    bf16, f32 = jnp.bfloat16, jnp.float32
    dma = pltpu.SemaphoreType.DMA
    vmem = pl.BlockSpec(memory_space=pltpu.VMEM)
    hbm = pl.BlockSpec(memory_space=pl.ANY)
    nxt, prior = pl.pallas_call(
        functools.partial(kernel, n, n_sec),
        out_shape=(jax.ShapeDtypeStruct((t, d), bf16), jax.ShapeDtypeStruct((t, d), bf16)),
        in_specs=[vmem] * 3 + [hbm] * 5,
        out_specs=(hbm, hbm),
        scratch_shapes=[
            pltpu.VMEM((t, d), bf16),
            pltpu.VMEM((t, d), bf16),
            pltpu.VMEM((d, h), bf16),
            pltpu.VMEM((d, h), bf16),
            pltpu.VMEM((h, d), bf16),
            pltpu.VMEM((n, CAP, d), bf16),
            pltpu.VMEM((n, CAP, d), bf16),
            pltpu.VMEM((2, n + 1, CAP, d), bf16),
            pltpu.VMEM((2, CAP, d), bf16),
            pltpu.VMEM((2, t, d), bf16),
            pltpu.VMEM((t, 128), f32),
            pltpu.VMEM((2, t, 128), f32),
            pltpu.VMEM((m, h), f32),
            pltpu.VMEM((m, h), f32),
            pltpu.VMEM((2, m, h), bf16),
            dma((5,)),
            dma((2, 2, n, PIECES)),
            dma((2, n, PIECES)),
            dma((2, n, nc)),
            dma((2, n + 1, nc)),
            dma((2, nc)),
            dma((2, nc)),
            dma((2,)),
            dma((2,)),
            dma((2,)),
            dma((2,)),
            dma((2, nc)),
        ],
        compiler_params=pltpu.CompilerParams(
            collective_id=0, has_side_effects=True, vmem_limit_bytes=58 * 1024 * 1024
        ),
        cost_estimate=pl.CostEstimate(
            flops=12 * m * d * h, bytes_accessed=6 * d * h + 8 * t * d, transcendentals=0
        ),
    )(
        expert_ids[0],
        slot_index[0],
        gate_scale[0],
        tokens[0],
        cotangent[0],
        gate_weight[0],
        up_weight[0],
        down_weight[0],
    )
    return nxt[None], prior[None]


def solution(mesh):
    rows = P("section", "expert", None)
    in_specs = (rows,) * 5 + (P("section", None, "expert"),) * 2 + (rows,)
    return jax.shard_map(
        functools.partial(body, mesh.shape["expert"], mesh.shape["section"]),
        mesh=mesh,
        in_specs=in_specs,
        out_specs=(rows, rows),
        check_vma=False,
    )
```

time: 242 us -> 199 us (0.82); the launches traced: 239 us -> 198 us
  Pallas kernels: 0 us -> 189 us
  waiting for transfers between devices: 167 us -> 0 us
  matrix products: 33.4 us -> 0 us
  between operations: 13.9 us -> 0.65 us
  other arithmetic: 8.83 us -> 0 us
  starting transfers between devices: 6.06 us -> 0 us
    pallas_call x0 -> x1, Pallas kernels: none -> 189 us  [body(): pl.pallas_call(functools.partial(kernel, n, n_sec), out_shape=(jax.ShapeD...]
    all_gather x2 -> x0, waiting for transfers between devices: 70.5 us -> none  [the longest x1 40.7 us: body(): piece = lax.all_gather(sent, 'expert', axis=0, tiled=True)]
    reduce_scatter x2 -> x0, waiting for transfers between devices: 61.5 us -> none  [the longest x1 36.8 us: body(): lax.psum_scatter((behind + jnp.dot(grad_up, up_mat.T, preferred_element_t...]
    ppermute x2 -> x0, waiting for transfers between devices: 35 us -> none  [from_behind(): return lax.ppermute(x, axis, pairs)]
    dot_general x8 -> x0, matrix products: 33.4 us -> none  [the longest x1 6.36 us: body(): jnp.dot(lax.all_gather(back, 'expert', axis=0, tiled=True), down_mat.T, p...]
    gather x2 -> x0, local copies, waits for them, and re-layouts: 6.92 us -> none  [the longest x1 3.47 us: body(): jnp.take(inward, slot, axis=0)]
    unnamed x14 -> x7, local copies, waits for them, and re-layouts: 2.49 us -> 8.45 us
    ppermute x2 -> x0, starting transfers between devices: 5.72 us -> none  [from_behind(): return lax.ppermute(x, axis, pairs)]
  transfers between devices with their start and end apart: 6 -> 0, of which waited for: 5 -> 0; matrix products, arithmetic and copies ran while one was open for 15% -> 0% of each run, Pallas kernels for 0% -> 0%
where the time goes in v1:
time: 199 us; the launch traced here: 198 us
  Pallas kernels  189 us (95%)
  local copies, waits for them, and re-layouts  8.45 us (4%)
    pallas_call x1, Pallas kernels, body(): pl.pallas_call(functools.partial(kernel, n, n_sec), out_shape=(jax.ShapeD...  189 us
    unnamed x7, local copies, waits for them, and re-layouts  8.45 us

profile of v1, /device:TPU:1, one launch (start us, length us, event | category | flops | bytes accessed | tf_op | source)
XLA Modules:
  0.0 198.5 jit_solution(12282869374187748704)
XLA Ops:
  0.6 1.4 copy.10
  2.0 1.4 copy.11
  3.5 1.4 copy.12
  4.9 189.4 %shard_map.95 = (bf16[128,7168]{1,0:T(8,128)(2,1)}, bf16[128,7168]{1,0:T(8,128)(2,1)}) custom-call(s32[128,8]{1,0:T(8,128)} %bitcast.17, s32[128,8]{1,0:T(8,128)} %bitcast.18, f32[128,8]{1,0:T(8,128)} %bitcast.19, bf16[128,7168]{1,0:T(8,128)(2,1)} %bitcast.13, bf16[128,7168]{1,0:T(8,128)(2,1)} %bitcast.14, bf16[7168,512]{1,0:T(8,128)(2,1)} %bitcast.10, ...), custom_call_target="tpu_custom_call" | custom-call | flops 5637144576 | bytes 29360128 | tf_op jit(solution)/shard_map/pallas_call | solution.py:387
  194.3 0.0 copy-start
  194.3 3.0 %copy.15 = bf16[1,128,7168]{2,1,0:T(8,128)(2,1)} copy(bf16[1,128,7168]{2,1,0:T(8,128)(2,1)} %bitcast.16) | data formatting | bytes 3670016
  197.2 0.0 copy-done
  197.2 1.2 copy.16
Async XLA Ops:
  194.3 3.0 %copy-start = (bf16[128,7168]{1,0:T(8,128)(2,1)S(1)}, bf16[128,7168]{1,0:T(8,128)(2,1)}, u32[]{:S(2)}) copy-start(bf16[128,7168]{1,0:T(8,128)(2,1)} %get-tuple-element.5) | copy-start | bytes 5505028

commit v2 on v1

v2 whole, which is shorter than its diff:
```python
import functools

import jax
import jax.numpy as jnp
from jax import lax
from jax.experimental import pallas as pl
from jax.experimental.pallas import tpu as pltpu
from jax.sharding import PartitionSpec as P

CAP = 32
CH = 1024
AHEAD = 2
MESH = pl.DeviceIdType.MESH
NT = (((1,), (1,)), ((), ()))
TN = (((0,), (0,)), ((), ()))


def kernel(
    n,
    n_sec,
    ids_ref,
    slots_ref,
    scale_ref,
    tok_hbm,
    cot_hbm,
    gw_hbm,
    uw_hbm,
    dw_hbm,
    next_hbm,
    prior_hbm,
    tok,
    cot,
    gw,
    uw,
    dw,
    rows_all,
    rs_in,
    fin,
    shift,
    route,
    route_in,
    gate,
    up,
    grad,
    hid,
    load_sem,
    ag_send,
    ag_recv,
    rs_send,
    rs_recv,
    fin_send,
    fin_recv,
    shift_send,
    shift_recv,
    route_send,
    route_recv,
    out_sem,
):
    f32, bf16 = jnp.float32, jnp.bfloat16
    sec = lax.axis_index("section")
    me = lax.axis_index("expert")
    d = tok.shape[1]
    nc = d // CH
    has_right, has_left = me < n - 1, me > 0
    has_next, has_prev = sec < n_sec - 1, sec > 0
    right = (sec, jnp.minimum(me + 1, n - 1))
    left = (sec, jnp.maximum(me - 1, 0))
    after = (jnp.minimum(sec + 1, n_sec - 1), me)
    before = (jnp.maximum(sec - 1, 0), me)
    neighbours = ((has_right, right), (has_left, left), (has_next, after), (has_prev, before))

    loads = [
        pltpu.make_async_copy(src, dst, load_sem.at[k])
        for k, (src, dst) in enumerate(
            ((tok_hbm, tok), (cot_hbm, cot), (gw_hbm, gw), (uw_hbm, uw), (dw_hbm, dw))
        )
    ]
    for load in loads:
        load.start()

    barrier = pltpu.get_barrier_semaphore()
    for exists, where in neighbours:

        @pl.when(exists)
        def _():
            pl.semaphore_signal(barrier, inc=1, device_id=where, device_id_type=MESH)

    def col(c):
        return pl.ds(pl.multiple_of(c * CH, CH), CH)

    hit = ids_ref[...] == sec
    slot = jnp.sum(jnp.where(hit, slots_ref[...], 0), axis=0, keepdims=True)
    weight = jnp.sum(jnp.where(hit, scale_ref[...], 0.0), axis=0, keepdims=True)
    chosen = jnp.sum(hit.astype(jnp.int32), axis=0, keepdims=True)
    place = lax.broadcasted_iota(jnp.int32, (128, hit.shape[1]), 0)
    picks = jnp.where((place == slot) & (chosen > 0), 1.0, 0.0)
    route[...] = jnp.transpose(jnp.where(place < CAP, picks, weight))

    def gather_own(a):
        @pl.loop(0, nc)
        def _(c):
            table = route[:, :CAP].astype(bf16)
            if a == 0:
                rows = tok[:, col(c)]
            else:
                rows = (route[:, CAP : CAP + 1] * cot[:, col(c)].astype(f32)).astype(bf16)
            got = lax.dot_general(table, rows, TN, preferred_element_type=f32)
            rows_all[a, me, :, col(c)] = got.astype(bf16)

    def ag_copy(u, j, way):
        ref = rows_all.at[u // nc, j, :, col(u % nc)]
        return pltpu.make_async_remote_copy(
            src_ref=ref,
            dst_ref=ref,
            send_sem=ag_send.at[u, way, j],
            recv_sem=ag_recv.at[u, j],
            device_id=(right, left)[way],
            device_id_type=MESH,
        )

    def ag_own(u):
        for way in range(2):

            @pl.when((has_right, has_left)[way])
            def _():
                ag_copy(u, me, way).start()

    def ag_step(u, s):
        for way, j, ok in ((0, me - s, me - s >= 0), (1, me + s, me + s < n)):

            @pl.when(ok)
            def _():
                ag_copy(u, j, way).wait_recv()
                if s < n - 1:

                    @pl.when((has_right, has_left)[way])
                    def _():
                        ag_copy(u, j, way).start()

    def ag_sent(u):
        for s in range(n - 1):
            for way, j, ok in ((0, me - s, me - s >= 0), (1, me + s, me + s < n)):

                @pl.when(ok & (has_right, has_left)[way])
                def _():
                    ag_copy(u, j, way).wait_send()

    def rs_copy(a, j, c, way):
        into = j if way == 0 else jnp.where(j == me - 1, n, j)
        return pltpu.make_async_remote_copy(
            src_ref=rows_all.at[a, j, :, col(c)],
            dst_ref=rs_in.at[a, into, :, col(c)],
            send_sem=rs_send.at[a, j, c],
            recv_sem=rs_recv.at[a, into, c],
            device_id=(right, left)[way],
            device_id_type=MESH,
        )

    def rs_take(a, j, into, c):
        pltpu.make_async_remote_copy(
            src_ref=rows_all.at[a, j, :, col(c)],
            dst_ref=rs_in.at[a, into, :, col(c)],
            send_sem=rs_send.at[a, j, c],
            recv_sem=rs_recv.at[a, into, c],
            device_id=right,
            device_id_type=MESH,
        ).wait_recv()
        total = rows_all[a, j, :, col(c)].astype(f32) + rs_in[a, into, :, col(c)].astype(f32)
        rows_all[a, j, :, col(c)] = total.astype(bf16)

    def fin_copy(a, c):
        return pltpu.make_async_remote_copy(
            src_ref=rows_all.at[a, me, :, col(c)],
            dst_ref=fin.at[a, :, col(c)],
            send_sem=fin_send.at[a, c],
            recv_sem=fin_recv.at[a, c],
            device_id=(after, before)[a],
            device_id_type=MESH,
        )

    def rs_step(a, b):
        for way in range(2):
            c = b - (me, n - 1 - me)[way]
            into = (me, n)[way]
            has_in = (has_left, has_right)[way]

            @pl.when((c >= 0) & (c < nc))
            def _():
                for s in range(n - 1):
                    j = (n - 1 - s, s)[way]

                    @pl.when((j > me, j < me)[way])
                    def _():
                        @pl.when(has_in)
                        def _():
                            rs_take(a, j, j, c)

                        rs_copy(a, j, c, way).start()

                @pl.when(has_in)
                def _():
                    rs_take(a, me, into, c)

        c = b - (n - 1)

        @pl.when((c >= 0) & (c < nc) & (has_next, has_prev)[a])
        def _():
            fin_copy(a, c).start()

    def rs_sent(a, c):
        for j in range(n):
            for way, ok in ((0, j > me), (1, j < me)):

                @pl.when(ok)
                def _():
                    rs_copy(a, j, c, way).wait_send()

        @pl.when((has_next, has_prev)[a])
        def _():
            fin_copy(a, c).wait_send()

    def shift_copy(a):
        return pltpu.make_async_remote_copy(
            src_ref=(tok, cot)[a],
            dst_ref=shift.at[a],
            send_sem=shift_send.at[a],
            recv_sem=shift_recv.at[a],
            device_id=(after, before)[a],
            device_id_type=MESH,
        )

    def route_copy(a):
        return pltpu.make_async_remote_copy(
            src_ref=route,
            dst_ref=route_in.at[a],
            send_sem=route_send.at[a],
            recv_sem=route_recv.at[a],
            device_id=(after, before)[a],
            device_id_type=MESH,
        )

    def out_copy(a, c):
        return pltpu.make_async_copy(
            shift.at[a, :, col(c)], (next_hbm, prior_hbm)[a].at[:, col(c)], out_sem.at[a, c]
        )

    sends_on = (has_next, has_prev)
    takes_from = (has_prev, has_next)

    def finish(a, c):
        @pl.when(takes_from[a])
        def _():
            fin_copy(a, c).wait_recv()
            table = route_in[a, :, :CAP].astype(bf16)
            rows = jnp.dot(table, fin[a, :, col(c)], preferred_element_type=f32)
            if a == 0:
                rows = route_in[a, :, CAP : CAP + 1] * rows
            shift[a, :, col(c)] = (shift[a, :, col(c)].astype(f32) + rows).astype(bf16)

        @pl.when(jnp.logical_not(takes_from[a]))
        def _():
            shift[a, :, col(c)] = jnp.zeros((shift.shape[1], CH), bf16)

        out_copy(a, c).start()

    loads[0].wait()
    gather_own(0)
    peers = sum(exists.astype(jnp.int32) for exists, _w in neighbours)
    pl.semaphore_wait(barrier, peers)

    for u in range(AHEAD):
        ag_own(u)
    loads[1].wait()
    gather_own(1)
    for a in range(2):

        @pl.when(sends_on[a])
        def _():
            route_copy(a).start()
            shift_copy(a).start()

    m = n * CAP
    gate[...] = jnp.zeros_like(gate)
    up[...] = jnp.zeros_like(up)
    grad[...] = jnp.zeros_like(grad)

    @pl.loop(0, 2 * nc + n - 1)
    def _(t):
        @pl.when(t + AHEAD < 2 * nc)
        def _():
            ag_own(t + AHEAD)

        for s in range(1, n):

            @pl.when((t >= s) & (t - s < 2 * nc))
            def _():
                ag_step(t - s, s)

        c = t - (n - 1)
        b = c - nc

        @pl.when(c == 0)
        def _():
            loads[2].wait()
            loads[3].wait()

        @pl.when((c >= 0) & (b < 0))
        def _():
            rows = rows_all[0, :, :, col(c)].reshape(m, CH)
            gate[...] += jnp.dot(rows, gw[col(c), :], preferred_element_type=f32)
            up[...] += jnp.dot(rows, uw[col(c), :], preferred_element_type=f32)

        @pl.when(b == 0)
        def _():
            g = gate[...]
            hid[0] = (g * jax.nn.sigmoid(g) * up[...]).astype(bf16)
            loads[4].wait()

        @pl.when(b >= 0)
        def _():
            ag_sent(b)
            part = jnp.dot(hid[0], dw[:, col(b)], preferred_element_type=f32)
            rows_all[0, :, :, col(b)] = part.astype(bf16).reshape(n, CAP, CH)
            rs_step(0, b)
            rows = rows_all[1, :, :, col(b)].reshape(m, CH)
            grad[...] += lax.dot_general(rows, dw[:, col(b)], NT, preferred_element_type=f32)

    g = gate[...]
    sig = jax.nn.sigmoid(g)
    hid[0] = (grad[...] * (g * sig)).astype(bf16)
    hid[1] = (grad[...] * up[...] * (sig * (1.0 + g * (1.0 - sig)))).astype(bf16)

    for a in range(2):

        @pl.when(takes_from[a])
        def _():
            route_copy(a).wait_recv()
            shift_copy(a).wait_recv()

    @pl.loop(0, nc + n)
    def _(b):
        @pl.when(b < nc)
        def _():
            ag_sent(nc + b)
            part = lax.dot_general(hid[1], gw[col(b), :], NT, preferred_element_type=f32)
            part += lax.dot_general(hid[0], uw[col(b), :], NT, preferred_element_type=f32)
            rows_all[1, :, :, col(b)] = part.astype(bf16).reshape(n, CAP, CH)

        rs_step(0, nc + b)
        rs_step(1, b)

        @pl.when(b < nc)
        def _():
            finish(0, b)

        @pl.when(b >= n)
        def _():
            finish(1, b - n)

    for a in range(2):

        @pl.when(sends_on[a])
        def _():
            route_copy(a).wait_send()
            shift_copy(a).wait_send()

    @pl.loop(0, nc)
    def _(c):
        for a in range(2):
            rs_sent(a, c)
            out_copy(a, c).wait()


def body(
    n, n_sec, tokens, cotangent, expert_ids, slot_index, gate_scale, gate_weight, up_weight, down_weight
):
    t, d = tokens.shape[1:]
    h = gate_weight.shape[2]
    nc = d // CH
    m = n * CAP
    bf16, f32 = jnp.bfloat16, jnp.float32
    dma = pltpu.SemaphoreType.DMA
    vmem = pl.BlockSpec(memory_space=pltpu.VMEM)
    hbm = pl.BlockSpec(memory_space=pl.ANY)
    nxt, prior = pl.pallas_call(
        functools.partial(kernel, n, n_sec),
        out_shape=(jax.ShapeDtypeStruct((t, d), bf16), jax.ShapeDtypeStruct((t, d), bf16)),
        in_specs=[vmem] * 3 + [hbm] * 5,
        out_specs=(hbm, hbm),
        scratch_shapes=[
            pltpu.VMEM((t, d), bf16),
            pltpu.VMEM((t, d), bf16),
            pltpu.VMEM((d, h), bf16),
            pltpu.VMEM((d, h), bf16),
            pltpu.VMEM((h, d), bf16),
            pltpu.VMEM((2, n, CAP, d), bf16),
            pltpu.VMEM((2, n + 1, CAP, d), bf16),
            pltpu.VMEM((2, CAP, d), bf16),
            pltpu.VMEM((2, t, d), bf16),
            pltpu.VMEM((t, 128), f32),
            pltpu.VMEM((2, t, 128), f32),
            pltpu.VMEM((m, h), f32),
            pltpu.VMEM((m, h), f32),
            pltpu.VMEM((m, h), f32),
            pltpu.VMEM((2, m, h), bf16),
            dma((5,)),
            dma((2 * nc, 2, n)),
            dma((2 * nc, n)),
            dma((2, n, nc)),
            dma((2, n + 1, nc)),
            dma((2, nc)),
            dma((2, nc)),
            dma((2,)),
            dma((2,)),
            dma((2,)),
            dma((2,)),
            dma((2, nc)),
        ],
        compiler_params=pltpu.CompilerParams(
            collective_id=0, has_side_effects=True, vmem_limit_bytes=58 * 1024 * 1024
        ),
        cost_estimate=pl.CostEstimate(
            flops=12 * m * d * h, bytes_accessed=6 * d * h + 8 * t * d, transcendentals=0
        ),
    )(
        expert_ids[0].T,
        slot_index[0].T,
        gate_scale[0].T,
        tokens[0],
        cotangent[0],
        gate_weight[0],
        up_weight[0],
        down_weight[0],
    )
    return nxt[None], prior[None]


def solution(mesh):
    rows = P("section", "expert", None)
    in_specs = (rows,) * 5 + (P("section", None, "expert"),) * 2 + (rows,)
    return jax.shard_map(
        functools.partial(body, mesh.shape["expert"], mesh.shape["section"]),
        mesh=mesh,
        in_specs=in_specs,
        out_specs=(rows, rows),
        check_vma=False,
    )
```

time: 199 us -> 130 us (0.65)
  Pallas kernels: 189 us -> 124 us
  local copies, waits for them, and re-layouts: 8.45 us -> 4.21 us
    pallas_call x1, Pallas kernels: 189 us -> 124 us  [body(): pl.pallas_call(functools.partial(kernel, n, n_sec), out_shape=(jax.ShapeD...]
    unnamed x7 -> x4, local copies, waits for them, and re-layouts: 8.45 us -> 4.21 us
where the time goes in v2:
time: 130 us; the launch traced here: 129 us
  Pallas kernels  124 us (95%)
  local copies, waits for them, and re-layouts  4.21 us (3%)
    pallas_call x1, Pallas kernels, body(): pl.pallas_call(functools.partial(kernel, n, n_sec), out_shape=(jax.ShapeD...  124 us
    unnamed x4, local copies, waits for them, and re-layouts  4.21 us

profile of v2, /device:TPU:1, one launch (start us, length us, event | category | flops | bytes accessed | tf_op | source)
XLA Modules:
  0.0 128.6 jit_solution(5440607965987753709)
XLA Ops:
  0.6 123.8 %shard_map.95 = (bf16[128,7168]{1,0:T(8,128)(2,1)}, bf16[128,7168]{1,0:T(8,128)(2,1)}) custom-call(s32[8,128]{1,0:T(8,128)} %bitcast.23, s32[8,128]{1,0:T(8,128)} %bitcast.24, f32[8,128]{1,0:T(8,128)} %bitcast.25, bf16[128,7168]{1,0:T(8,128)(2,1)} %bitcast.19, bf16[128,7168]{1,0:T(8,128)(2,1)} %bitcast.20, bf16[7168,512]{1,0:T(8,128)(2,1)} %bitcast.16, ...), custom_call_target="tpu_custom_call" | custom-call | flops 5637144576 | bytes 29360128 | tf_op jit(solution)/shard_map/pallas_call | solution.py:385
  124.4 0.0 copy-start
  124.4 3.0 %copy.12 = bf16[1,128,7168]{2,1,0:T(8,128)(2,1)} copy(bf16[1,128,7168]{2,1,0:T(8,128)(2,1)} %bitcast.22) | data formatting | bytes 3670016
  127.4 0.0 copy-done
  127.4 1.2 copy.13
Async XLA Ops:
  124.4 3.0 %copy-start = (bf16[128,7168]{1,0:T(8,128)(2,1)S(1)}, bf16[128,7168]{1,0:T(8,128)(2,1)}, u32[]{:S(2)}) copy-start(bf16[128,7168]{1,0:T(8,128)(2,1)} %get-tuple-element.5) | copy-start | bytes 5505028

commit v3 on v2

--- a/solution.py
+++ b/solution.py
@@ -8,9 +8,12 @@
 from jax.sharding import PartitionSpec as P
 
 CAP = 32
-CH = 1024
-AHEAD = 2
+AHEAD = 4
 MESH = pl.DeviceIdType.MESH
+def chunk_width(n):
+    return 512 if n <= 4 else 1024
+
+
 NT = (((1,), (1,)), ((), ()))
 TN = (((0,), (0,)), ((), ()))
 
@@ -60,7 +63,8 @@
     sec = lax.axis_index("section")
     me = lax.axis_index("expert")
     d = tok.shape[1]
-    nc = d // CH
+    ch = chunk_width(n)
+    nc = d // ch
     has_right, has_left = me < n - 1, me > 0
     has_next, has_prev = sec < n_sec - 1, sec > 0
     right = (sec, jnp.minimum(me + 1, n - 1))
@@ -86,7 +90,7 @@
             pl.semaphore_signal(barrier, inc=1, device_id=where, device_id_type=MESH)
 
     def col(c):
-        return pl.ds(pl.multiple_of(c * CH, CH), CH)
+        return pl.ds(pl.multiple_of(c * ch, ch), ch)
 
     hit = ids_ref[...] == sec
     slot = jnp.sum(jnp.where(hit, slots_ref[...], 0), axis=0, keepdims=True)
@@ -259,7 +263,7 @@
 
         @pl.when(jnp.logical_not(takes_from[a]))
         def _():
-            shift[a, :, col(c)] = jnp.zeros((shift.shape[1], CH), bf16)
+            shift[a, :, col(c)] = jnp.zeros((shift.shape[1], ch), bf16)
 
         out_copy(a, c).start()
 
@@ -306,7 +310,7 @@
 
         @pl.when((c >= 0) & (b < 0))
         def _():
-            rows = rows_all[0, :, :, col(c)].reshape(m, CH)
+            rows = rows_all[0, :, :, col(c)].reshape(m, ch)
             gate[...] += jnp.dot(rows, gw[col(c), :], preferred_element_type=f32)
             up[...] += jnp.dot(rows, uw[col(c), :], preferred_element_type=f32)
 
@@ -320,9 +324,9 @@
         def _():
             ag_sent(b)
             part = jnp.dot(hid[0], dw[:, col(b)], preferred_element_type=f32)
-            rows_all[0, :, :, col(b)] = part.astype(bf16).reshape(n, CAP, CH)
+            rows_all[0, :, :, col(b)] = part.astype(bf16).reshape(n, CAP, ch)
             rs_step(0, b)
-            rows = rows_all[1, :, :, col(b)].reshape(m, CH)
+            rows = rows_all[1, :, :, col(b)].reshape(m, ch)
             grad[...] += lax.dot_general(rows, dw[:, col(b)], NT, preferred_element_type=f32)
 
     g = gate[...]
@@ -344,7 +348,7 @@
             ag_sent(nc + b)
             part = lax.dot_general(hid[1], gw[col(b), :], NT, preferred_element_type=f32)
             part += lax.dot_general(hid[0], uw[col(b), :], NT, preferred_element_type=f32)
-            rows_all[1, :, :, col(b)] = part.astype(bf16).reshape(n, CAP, CH)
+            rows_all[1, :, :, col(b)] = part.astype(bf16).reshape(n, CAP, ch)
 
         rs_step(0, nc + b)
         rs_step(1, b)
@@ -376,7 +380,7 @@
 ):
     t, d = tokens.shape[1:]
     h = gate_weight.shape[2]
-    nc = d // CH
+    nc = d // chunk_width(n)
     m = n * CAP
     bf16, f32 = jnp.bfloat16, jnp.float32
     dma = pltpu.SemaphoreType.DMA

time: 130 us -> 151 us (1.16)
  Pallas kernels: 124 us -> 146 us
    pallas_call x1, Pallas kernels: 124 us -> 146 us  [body(): pl.pallas_call(functools.partial(kernel, n, n_sec), out_shape=(jax.ShapeD...]
where the time goes in v3:
time: 151 us
  Pallas kernels  146 us (97%)
  local copies, waits for them, and re-layouts  4.21 us (3%)
    pallas_call x1, Pallas kernels, body(): pl.pallas_call(functools.partial(kernel, n, n_sec), out_shape=(jax.ShapeD...  146 us
    unnamed x4, local copies, waits for them, and re-layouts  4.21 us

profile of v3, /device:TPU:1, one launch (start us, length us, event | category | flops | bytes accessed | tf_op | source)
XLA Modules:
  0.0 150.8 jit_solution(15610937503300617695)
XLA Ops:
  0.6 145.9 %shard_map.95 = (bf16[128,7168]{1,0:T(8,128)(2,1)}, bf16[128,7168]{1,0:T(8,128)(2,1)}) custom-call(s32[8,128]{1,0:T(8,128)} %bitcast.23, s32[8,128]{1,0:T(8,128)} %bitcast.24, f32[8,128]{1,0:T(8,128)} %bitcast.25, bf16[128,7168]{1,0:T(8,128)(2,1)} %bitcast.19, bf16[128,7168]{1,0:T(8,128)(2,1)} %bitcast.20, bf16[7168,512]{1,0:T(8,128)(2,1)} %bitcast.16, ...), custom_call_target="tpu_custom_call" | custom-call | flops 5637144576 | bytes 29360128 | tf_op jit(solution)/shard_map/pallas_call | solution.py:389
  146.5 0.0 copy-start
  146.5 3.0 %copy.12 = bf16[1,128,7168]{2,1,0:T(8,128)(2,1)} copy(bf16[1,128,7168]{2,1,0:T(8,128)(2,1)} %bitcast.22) | data formatting | bytes 3670016
  149.5 0.0 copy-done
  149.5 1.2 copy.13
Async XLA Ops:
  146.5 3.0 %copy-start = (bf16[128,7168]{1,0:T(8,128)(2,1)S(1)}, bf16[128,7168]{1,0:T(8,128)(2,1)}, u32[]{:S(2)}) copy-start(bf16[128,7168]{1,0:T(8,128)(2,1)} %get-tuple-element.5) | copy-start | bytes 5505028

commit v4 on v2

--- a/solution.py
+++ b/solution.py
@@ -12,33 +12,30 @@
 AHEAD = 2
 MESH = pl.DeviceIdType.MESH
 NT = (((1,), (1,)), ((), ()))
-TN = (((0,), (0,)), ((), ()))
 
 
 def kernel(
     n,
     n_sec,
-    ids_ref,
-    slots_ref,
-    scale_ref,
-    tok_hbm,
-    cot_hbm,
+    sent_hbm,
+    back_hbm,
+    route,
+    tok,
+    cot,
     gw_hbm,
     uw_hbm,
     dw_hbm,
-    next_hbm,
-    prior_hbm,
-    tok,
-    cot,
+    shift0,
+    shift1,
+    route0,
+    route1,
+    fin0,
+    fin1,
     gw,
     uw,
     dw,
     rows_all,
     rs_in,
-    fin,
-    shift,
-    route,
-    route_in,
     gate,
     up,
     grad,
@@ -54,12 +51,11 @@
     shift_recv,
     route_send,
     route_recv,
-    out_sem,
 ):
     f32, bf16 = jnp.float32, jnp.bfloat16
     sec = lax.axis_index("section")
     me = lax.axis_index("expert")
-    d = tok.shape[1]
+    d = gw.shape[0]
     nc = d // CH
     has_right, has_left = me < n - 1, me > 0
     has_next, has_prev = sec < n_sec - 1, sec > 0
@@ -72,7 +68,13 @@
     loads = [
         pltpu.make_async_copy(src, dst, load_sem.at[k])
         for k, (src, dst) in enumerate(
-            ((tok_hbm, tok), (cot_hbm, cot), (gw_hbm, gw), (uw_hbm, uw), (dw_hbm, dw))
+            (
+                (sent_hbm, rows_all.at[0, me]),
+                (back_hbm, rows_all.at[1, me]),
+                (gw_hbm, gw),
+                (uw_hbm, uw),
+                (dw_hbm, dw),
+            )
         )
     ]
     for load in loads:
@@ -87,25 +89,6 @@
 
     def col(c):
         return pl.ds(pl.multiple_of(c * CH, CH), CH)
-
-    hit = ids_ref[...] == sec
-    slot = jnp.sum(jnp.where(hit, slots_ref[...], 0), axis=0, keepdims=True)
-    weight = jnp.sum(jnp.where(hit, scale_ref[...], 0.0), axis=0, keepdims=True)
-    chosen = jnp.sum(hit.astype(jnp.int32), axis=0, keepdims=True)
-    place = lax.broadcasted_iota(jnp.int32, (128, hit.shape[1]), 0)
-    picks = jnp.where((place == slot) & (chosen > 0), 1.0, 0.0)
-    route[...] = jnp.transpose(jnp.where(place < CAP, picks, weight))
-
-    def gather_own(a):
-        @pl.loop(0, nc)
-        def _(c):
-            table = route[:, :CAP].astype(bf16)
-            if a == 0:
-                rows = tok[:, col(c)]
-            else:
-                rows = (route[:, CAP : CAP + 1] * cot[:, col(c)].astype(f32)).astype(bf16)
-            got = lax.dot_general(table, rows, TN, preferred_element_type=f32)
-            rows_all[a, me, :, col(c)] = got.astype(bf16)
 
     def ag_copy(u, j, way):
         ref = rows_all.at[u // nc, j, :, col(u % nc)]
@@ -171,7 +154,7 @@
     def fin_copy(a, c):
         return pltpu.make_async_remote_copy(
             src_ref=rows_all.at[a, me, :, col(c)],
-            dst_ref=fin.at[a, :, col(c)],
+            dst_ref=(fin0, fin1)[a].at[:, col(c)],
             send_sem=fin_send.at[a, c],
             recv_sem=fin_recv.at[a, c],
             device_id=(after, before)[a],
@@ -222,7 +205,7 @@
     def shift_copy(a):
         return pltpu.make_async_remote_copy(
             src_ref=(tok, cot)[a],
-            dst_ref=shift.at[a],
+            dst_ref=(shift0, shift1)[a],
             send_sem=shift_send.at[a],
             recv_sem=shift_recv.at[a],
             device_id=(after, before)[a],
@@ -232,46 +215,23 @@
     def route_copy(a):
         return pltpu.make_async_remote_copy(
             src_ref=route,
-            dst_ref=route_in.at[a],
+            dst_ref=(route0, route1)[a],
             send_sem=route_send.at[a],
             recv_sem=route_recv.at[a],
             device_id=(after, before)[a],
             device_id_type=MESH,
         )
 
-    def out_copy(a, c):
-        return pltpu.make_async_copy(
-            shift.at[a, :, col(c)], (next_hbm, prior_hbm)[a].at[:, col(c)], out_sem.at[a, c]
-        )
-
     sends_on = (has_next, has_prev)
     takes_from = (has_prev, has_next)
 
-    def finish(a, c):
-        @pl.when(takes_from[a])
-        def _():
-            fin_copy(a, c).wait_recv()
-            table = route_in[a, :, :CAP].astype(bf16)
-            rows = jnp.dot(table, fin[a, :, col(c)], preferred_element_type=f32)
-            if a == 0:
-                rows = route_in[a, :, CAP : CAP + 1] * rows
-            shift[a, :, col(c)] = (shift[a, :, col(c)].astype(f32) + rows).astype(bf16)
-
-        @pl.when(jnp.logical_not(takes_from[a]))
-        def _():
-            shift[a, :, col(c)] = jnp.zeros((shift.shape[1], CH), bf16)
-
-        out_copy(a, c).start()
-
     loads[0].wait()
-    gather_own(0)
+    loads[1].wait()
     peers = sum(exists.astype(jnp.int32) for exists, _w in neighbours)
     pl.semaphore_wait(barrier, peers)
 
     for u in range(AHEAD):
         ag_own(u)
-    loads[1].wait()
-    gather_own(1)
     for a in range(2):
 
         @pl.when(sends_on[a])
@@ -330,14 +290,7 @@
     hid[0] = (grad[...] * (g * sig)).astype(bf16)
     hid[1] = (grad[...] * up[...] * (sig * (1.0 + g * (1.0 - sig)))).astype(bf16)
 
-    for a in range(2):
-
-        @pl.when(takes_from[a])
-        def _():
-            route_copy(a).wait_recv()
-            shift_copy(a).wait_recv()
-
-    @pl.loop(0, nc + n)
+    @pl.loop(0, nc + n - 1)
     def _(b):
         @pl.when(b < nc)
         def _():
@@ -349,26 +302,26 @@
         rs_step(0, nc + b)
         rs_step(1, b)
 
-        @pl.when(b < nc)
-        def _():
-            finish(0, b)
-
-        @pl.when(b >= n)
-        def _():
-            finish(1, b - n)
-
     for a in range(2):
 
         @pl.when(sends_on[a])
         def _():
             route_copy(a).wait_send()
             shift_copy(a).wait_send()
+
+        @pl.when(takes_from[a])
+        def _():
+            route_copy(a).wait_recv()
+            shift_copy(a).wait_recv()
 
     @pl.loop(0, nc)
     def _(c):
         for a in range(2):
             rs_sent(a, c)
-            out_copy(a, c).wait()
+
+            @pl.when(takes_from[a])
+            def _():
+                fin_copy(a, c).wait_recv()
 
 
 def body(
@@ -380,25 +333,33 @@
     m = n * CAP
     bf16, f32 = jnp.bfloat16, jnp.float32
     dma = pltpu.SemaphoreType.DMA
-    vmem = pl.BlockSpec(memory_space=pltpu.VMEM)
     hbm = pl.BlockSpec(memory_space=pl.ANY)
-    nxt, prior = pl.pallas_call(
+    section = lax.axis_index("section")
+    hit = expert_ids[0] == section
+    slot = jnp.sum(jnp.where(hit, slot_index[0], 0), axis=1)
+    weight = jnp.sum(jnp.where(hit, gate_scale[0], jnp.float32(0.0)), axis=1)
+    place = jnp.where(jnp.any(hit, axis=1), slot, CAP)
+    table = (jnp.arange(CAP, dtype=jnp.int32)[:, None] == place[None, :]).astype(bf16)
+    sent = jnp.dot(table, tokens[0], preferred_element_type=f32).astype(bf16)
+    carried = (weight[:, None] * cotangent[0].astype(f32)).astype(bf16)
+    back = jnp.dot(table, carried, preferred_element_type=f32).astype(bf16)
+    lane = jnp.arange(128, dtype=jnp.int32)[None, :]
+    picks = (lane == place[:, None]).astype(f32)
+    route = jnp.where(lane < CAP, picks, weight[:, None])
+    shape = jax.ShapeDtypeStruct
+    tok_in, cot_in, route0, route1, fin0, fin1 = pl.pallas_call(
         functools.partial(kernel, n, n_sec),
-        out_shape=(jax.ShapeDtypeStruct((t, d), bf16), jax.ShapeDtypeStruct((t, d), bf16)),
-        in_specs=[vmem] * 3 + [hbm] * 5,
-        out_specs=(hbm, hbm),
+        out_shape=(shape((t, d), bf16),) * 2
+        + (shape((t, 128), f32),) * 2
+        + (shape((CAP, d), bf16),) * 2,
+        in_specs=[hbm] * 8,
+        out_specs=(hbm,) * 6,
         scratch_shapes=[
-            pltpu.VMEM((t, d), bf16),
-            pltpu.VMEM((t, d), bf16),
             pltpu.VMEM((d, h), bf16),
             pltpu.VMEM((d, h), bf16),
             pltpu.VMEM((h, d), bf16),
             pltpu.VMEM((2, n, CAP, d), bf16),
             pltpu.VMEM((2, n + 1, CAP, d), bf16),
-            pltpu.VMEM((2, CAP, d), bf16),
-            pltpu.VMEM((2, t, d), bf16),
-            pltpu.VMEM((t, 128), f32),
-            pltpu.VMEM((2, t, 128), f32),
             pltpu.VMEM((m, h), f32),
             pltpu.VMEM((m, h), f32),
             pltpu.VMEM((m, h), f32),
@@ -414,7 +375,6 @@
             dma((2,)),
             dma((2,)),
             dma((2,)),
-            dma((2, nc)),
         ],
         compiler_params=pltpu.CompilerParams(
             collective_id=0, has_side_effects=True, vmem_limit_bytes=58 * 1024 * 1024
@@ -423,15 +383,24 @@
             flops=12 * m * d * h, bytes_accessed=6 * d * h + 8 * t * d, transcendentals=0
         ),
     )(
-        expert_ids[0].T,
-        slot_index[0].T,
-        gate_scale[0].T,
+        sent,
+        back,
+        route,
         tokens[0],
         cotangent[0],
         gate_weight[0],
         up_weight[0],
         down_weight[0],
     )
+
+    def place_rows(base, rows, source):
+        got = jnp.dot(source[:, :CAP].astype(bf16), rows, preferred_element_type=f32)
+        return base.astype(f32), got, source[:, CAP : CAP + 1]
+
+    base, got, scale = place_rows(tok_in, fin0, route0)
+    nxt = jnp.where(section > 0, base + scale * got, 0.0).astype(bf16)
+    base, got, _ = place_rows(cot_in, fin1, route1)
+    prior = jnp.where(section < n_sec - 1, base + got, 0.0).astype(bf16)
     return nxt[None], prior[None]
 
 

time: 130 us -> 137 us (1.054)
  matrix products: 0 us -> 11 us
  local copies, waits for them, and re-layouts: 4.21 us -> 0.18 us
  other arithmetic: 0 us -> 2.18 us
    dot_general x0 -> x4, matrix products: none -> 11 us  [the longest x2 5.63 us: place_rows(): jnp.dot(source[:, :CAP].astype(bf16), rows, preferred_element_type=f32)]
    unnamed x4 -> x6, local copies, waits for them, and re-layouts: 4.21 us -> 0.01 us
    reduce_sum x0 -> x2, other arithmetic: none -> 1.42 us  [the longest x1 0.72 us: body(): weight = jnp.sum(jnp.where(hit, gate_scale[0], jnp.float32(0.0)), axis=1)]
where the time goes in v4:
time: 137 us
  Pallas kernels  123 us (90%)
  matrix products  11 us (8%)
  other arithmetic  2.18 us (2%)
    pallas_call x1, Pallas kernels, body(): pl.pallas_call(functools.partial(kernel, n, n_sec), out_shape=(shape((t,...  123 us
    dot_general x2, matrix products, place_rows(): jnp.dot(source[:, :CAP].astype(bf16), rows, preferred_element_type=f32)  5.63 us
    dot_general x1, matrix products, body(): back = jnp.dot(table, carried, preferred_element_type=f32).astype(bf16)  2.78 us

profile of v4, /device:TPU:1, one launch (start us, length us, event | category | flops | bytes accessed | tf_op | source)
XLA Modules:
  0.0 136.7 jit_solution(12448581514542861288)
XLA Ops:
  0.6 0.7 select_reduce_fusion
  1.4 0.7 select_reduce_fusion.1
  2.1 2.8 %convolution_convert_fusion.back_hbm = bf16[32,7168]{1,0:T(8,128)(2,1)} fusion(f32[128]{0:T(128)S(1)} %get-tuple-element.14, s32[128]{0:T(128)S(1)} %broadcast_select_fusion, bf16[1,128,7168]{2,1,0:T(8,128)(2,1)} %param.9), kind=kOutput, calls=%fused_computation.9 | convolution fusion | flops 61706240 | bytes 2294784 | tf_op jit(solution)/shard_map/dot_general | solution.py:345
  4.9 0.7 convert_select_fusion.route
  5.6 2.6 %convolution_convert_fusion.1.sent_hbm = bf16[32,7168]{1,0:T(8,128)(2,1)} fusion(s32[128]{0:T(128)S(1)} %broadcast_select_fusion, bf16[1,128,7168]{2,1,0:T(8,128)(2,1)} %param.8), kind=kOutput, calls=%fused_computation.10 | convolution fusion | flops 58953728 | bytes 2294272 | tf_op jit(solution)/shard_map/dot_general | solution.py:343
  8.2 122.6 %shard_map.95 = (bf16[128,7168]{1,0:T(8,128)(2,1)}, bf16[128,7168]{1,0:T(8,128)(2,1)}, f32[128,128]{1,0:T(8,128)}, f32[128,128]{1,0:T(8,128)}, bf16[32,7168]{1,0:T(8,128)(2,1)}, /*index=5*/bf16[32,7168]{1,0:T(8,128)(2,1)}) custom-call(bf16[32,7168]{1,0:T(8,128)(2,1)} %convolution_convert_fusion.1.sent_hbm, ...), custom_call_target="tpu_custom_call" | custom-call | flops 5637144576 | bytes 29360128 | tf_op jit(solution)/shard_map/pallas_call | solution.py:350
  130.8 0.0 copy-start
  130.8 0.0 copy-start.1
  130.8 0.0 copy-start.2
  130.8 3.7 %fusion.5 = bf16[1,128,7168]{2,1,0:T(8,128)(2,1)} fusion(bf16[32,7168]{1,0:T(8,128)(2,1)} %get-tuple-element.13, bf16[128,7168]{1,0:T(8,128)(2,1)} %get-tuple-element.11, pred[]{:T(512)S(6)} %lt.13, f32[128,128]{1,0:T(8,128)} %get-tuple-element.12), kind=kOutput, calls=%fused_computation.7 | convolution fusion | flops 62390272 | bytes 4161537 | tf_op jit(solution)/shard_map/dot_general | solution.py:397
  134.5 0.0 copy-done
  134.5 0.2 slice_reduce_fusion
  134.7 0.0 copy-done.1
  134.7 0.0 copy-done.2
  134.7 2.0 %fusion.6 = bf16[1,128,7168]{2,1,0:T(8,128)(2,1)} fusion(bf16[32,7168]{1,0:T(8,128)(2,1)S(1)} %copy-done.2, bf16[128,7168]{1,0:T(8,128)(2,1)S(1)} %copy-done.1, f32[128]{0:T(128)S(1)} %slice_reduce_fusion, pred[]{:T(512)S(6)} %gt.3, f32[128,128]{1,0:T(8,128)S(1)} %copy-done), kind=kOutput, calls=%fused_computation.8 | convolution fusion | flops 63307776 | bytes 4162049 | tf_op jit(solution)/shard_map/dot_general | solution.py:397
  (3 shorter events, 0.0 us)
Async XLA Ops:
  130.8 3.7 %copy-start = (f32[128,128]{1,0:T(8,128)S(1)}, f32[128,128]{1,0:T(8,128)}, u32[]{:S(2)}) copy-start(f32[128,128]{1,0:T(8,128)} %get-tuple-element.9) | copy-start | bytes 196612
  130.8 3.9 %copy-start.1 = (bf16[128,7168]{1,0:T(8,128)(2,1)S(1)}, bf16[128,7168]{1,0:T(8,128)(2,1)}, u32[]{:S(2)}) copy-start(bf16[128,7168]{1,0:T(8,128)(2,1)} %get-tuple-element.8) | copy-start | bytes 5505028
  130.8 3.9 %copy-start.2 = (bf16[32,7168]{1,0:T(8,128)(2,1)S(1)}, bf16[32,7168]{1,0:T(8,128)(2,1)}, u32[]{:S(2)}) copy-start(bf16[32,7168]{1,0:T(8,128)(2,1)} %get-tuple-element.10) | copy-start | bytes 1376260
